TPU v7x, 1024 devices: a whole 4x8x16 slice. The times are simulated.
1024 devices in a mesh: dp: 64 (over y, x, core), expert: 16 (over z).
Axes of the slice: x: 4, y: 8, z: 16, core: 2. Of those that a mesh axis runs over, the one named last changes fastest.
Arguments:
- grad_out: bfloat16 [1024, 3200], P('expert', 'dp'), may hold values from -6 to 6
- expert_index: int32 [1024], P('expert'), may hold values from 0 to 15, as said below
- slot_index: int32 [1024], P('expert'), may hold values from 0 to 4, as said below
- capacity: int32 [16], replicated, may hold values from 2 to 5, as said below
- router_share: float32 [1024], P('expert'), may hold values from 0.2 to 1
- routed_gate: bfloat16 [16, 80, 9216], P('expert', None, 'dp'), may hold values from -6 to 6
- routed_up: bfloat16 [16, 80, 9216], P('expert', None, 'dp'), may hold values from -6 to 6
- gate_weight: bfloat16 [16, 9216, 3200], P('expert', 'dp'), may hold values from -0.3125 to 0.3125
- up_weight: bfloat16 [16, 9216, 3200], P('expert', 'dp'), may hold values from -0.3125 to 0.3125
- down_weight: bfloat16 [16, 9216, 3200], P('expert', 'dp'), may hold values from -0.0625 to 0.0625
- shared_gate: bfloat16 [1024, 9216], P('expert', 'dp'), may hold values from -6 to 6
- shared_up: bfloat16 [1024, 9216], P('expert', 'dp'), may hold values from -6 to 6
- gate_common: bfloat16 [9216, 3200], P('dp'), may hold values from -0.3125 to 0.3125
- up_common: bfloat16 [9216, 3200], P('dp'), may hold values from -0.3125 to 0.3125
- down_common: bfloat16 [9216, 3200], P('dp'), may hold values from -0.0625 to 0.0625
Outputs:
- input_grad: bfloat16 [1024, 3200], P('expert', 'dp')
Inputs may be any that keep to these rules, and one draw needn't show every extreme that they name: `expert_index`: in each block of 64 tokens no expert is named more than 5 times, and one expert, the same in every block, is named exactly 5 times in every block. `slot_index`: the rank of the token among the tokens of its block that name the same expert, counted in token order from 0. The expert that is named 5 times in every block has capacity 5.
All inputs are finite; a program needn't handle non-finite values.
Results may differ from a plain program's by a relative error of at most 0.0052.
Values may be sent and summed in bfloat16 or wider, within the bound.
A program may use at most 32 MiB of HBM per device.

v0:
```python
import jax
import jax.numpy as jnp
from jax import lax
from jax.sharding import PartitionSpec as P


def silu_grads(grad_hidden, gate_pre, up_pre):
    gate_val = gate_pre.astype(jnp.float32)
    up_val = up_pre.astype(jnp.float32)
    sigmoid_gate = jax.nn.sigmoid(gate_val)
    grad_gate = grad_hidden * up_val * sigmoid_gate * (1.0 + gate_val * (1.0 - sigmoid_gate))
    grad_up = grad_hidden * gate_val * sigmoid_gate
    return (grad_gate.astype(jnp.bfloat16), grad_up.astype(jnp.bfloat16))


def back_through(grad_rows, gate_pre, up_pre, gate_mat, up_mat, down_mat):
    grad_hidden = lax.dot_general(
        grad_rows, down_mat, (((1,), (1,)), ((), ())), preferred_element_type=jnp.float32
    )
    grad_gate, grad_up = silu_grads(grad_hidden, gate_pre, up_pre)
    first_term = jnp.dot(grad_gate, gate_mat, preferred_element_type=jnp.float32)
    second_term = jnp.dot(grad_up, up_mat, preferred_element_type=jnp.float32)
    return first_term + second_term


def body(
    grad_out,
    expert_index,
    slot_index,
    capacity,
    router_share,
    routed_gate,
    routed_up,
    gate_weight,
    up_weight,
    down_weight,
    shared_gate,
    shared_up,
    gate_common,
    up_common,
    down_common,
):
    expert_count = capacity.shape[0]
    slot_count = routed_gate.shape[1] // expert_count
    onehot_cap = expert_index[:, None] == jnp.arange(expert_count, dtype=jnp.int32)[None, :]
    token_cap = jnp.sum(jnp.where(onehot_cap, capacity[None, :], 0), axis=1)
    keep_mask = slot_index < token_cap
    target_row = expert_index * slot_count + slot_index
    placing = (
        jnp.arange(expert_count * slot_count, dtype=jnp.int32)[:, None] == target_row[None, :]
    ) & keep_mask[None, :]
    place_half = placing.astype(jnp.bfloat16)
    share_col = router_share[:, None]
    full_rows = lax.all_gather(grad_out, "dp", axis=1, tiled=True)
    scaled = (share_col * full_rows.astype(jnp.float32)).astype(jnp.bfloat16)
    sent_rows = jnp.dot(place_half, scaled, preferred_element_type=jnp.float32).astype(jnp.bfloat16)
    arrived = lax.all_to_all(
        sent_rows.reshape(expert_count, slot_count, full_rows.shape[1]),
        "expert",
        split_axis=0,
        concat_axis=0,
        tiled=True,
    )
    width = full_rows.shape[1]
    routed_part = back_through(
        arrived.reshape(expert_count * slot_count, width),
        routed_gate[0],
        routed_up[0],
        gate_weight[0],
        up_weight[0],
        down_weight[0],
    )
    shared_part = back_through(
        full_rows, shared_gate, shared_up, gate_common, up_common, down_common
    )
    routed_cols, shared_cols = (
        lax.psum_scatter(routed_part, "dp", scatter_dimension=1, tiled=True),
        lax.psum_scatter(shared_part, "dp", scatter_dimension=1, tiled=True),
    )
    returned = lax.all_to_all(
        routed_cols.reshape(expert_count, slot_count, routed_cols.shape[1]),
        "expert",
        split_axis=0,
        concat_axis=0,
        tiled=True,
    )
    picked = jnp.take(
        returned.reshape(expert_count * slot_count, routed_cols.shape[1]), target_row, axis=0
    )
    total_grad = shared_cols + jnp.where(keep_mask[:, None], picked, 0.0)
    return total_grad.astype(jnp.bfloat16)


def solution(mesh):
    return jax.shard_map(
        body,
        mesh=mesh,
        in_specs=(
            P("expert", "dp"),
            P("expert"),
            P("expert"),
            P(),
            P("expert"),
            P("expert", None, "dp"),
            P("expert", None, "dp"),
            P("expert", "dp", None),
            P("expert", "dp", None),
            P("expert", "dp", None),
            P("expert", "dp"),
            P("expert", "dp"),
            P("dp", None),
            P("dp", None),
            P("dp", None),
        ),
        out_specs=P("expert", "dp"),
        check_vma=False,
    )
```

profile of v0, /device:TPU:1, one launch (start us, length us, event | category | flops | bytes accessed | tf_op | source)
XLA Modules:
  0.0 362.4 jit_solution(7774535255136612585)
XLA Ops:
  0.0 61.9 %all-gather = bf16[64,50,64]{2,1,0:T(8,128)(2,1)S(1)} all-gather(bf16[1,50,64]{2,1,0:T(8,128)(2,1)} %bitcast.39), channel_id=1, replica_groups=mesh['dp'=64,'expert'=16] {'dp'}, dimensions={0}, use_global_device_ids=true | all-gather | bytes 416000 | tf_op jit(solution)/shard_map/all_gather | solution.py:54
  64.3 9.6 %all-to-all-start = ((bf16[16,5,3200]{2,1,0:T(8,128)(2,1)}), bf16[16,5,3200]{2,1,0:T(8,128)(2,1)S(1)}, u32[]{:S(2)}, u32[]{:S(2)}) async-start(bf16[16,5,3200]{2,1,0:T(8,128)(2,1)} %reshape.27), calls=%async_computation | async-start | bytes 1638400 | tf_op jit(solution)/shard_map/all_to_all | solution.py:57
  73.9 1.8 fusion.47
  77.7 33.1 %all-to-all-done = bf16[16,5,3200]{2,1,0:T(8,128)(2,1)S(1)} async-done(((bf16[16,5,3200]{2,1,0:T(8,128)(2,1)}), bf16[16,5,3200]{2,1,0:T(8,128)(2,1)S(1)}, u32[]{:S(2)}, u32[]{:S(2)}) %all-to-all-start) | async-done | bytes 512032 | tf_op jit(solution)/shard_map/all_to_all | solution.py:57
  111.8 1.7 fusion.5
  114.7 2.0 convolution_add_fusion
  116.7 149.8 %fusion.46 = (f32[64,64]{0,1:T(8,128)S(1)}, f32[80,64]{0,1:T(8,128)S(1)}) fusion(f32[64,3200]{0,1:T(8,128)S(1)} %convolution_add_fusion.1, f32[80,3200]{0,1:T(8,128)} %convolution_add_fusion), kind=kCustom, calls=%all-reduce-scatter.2 | all-reduce-scatter fusion | flops 589825 | bytes 1884160
  266.5 1.9 collective-permute-start.14
  273.7 10.1 %collective-permute-start.18 = (f32[80,64]{0,1:T(8,128)S(1)}, f32[80,64]{0,1:T(8,128)S(1)}, u32[]{:S(2)}, u32[]{:S(2)}) collective-permute-start(f32[80,64]{0,1:T(8,128)S(1)} %get-tuple-element.8), channel_id=1, source_target_pairs={{0,80},{16,96},{32,112},{48,128},{64,144},{80,160},{96,176},{112,1... | collective-permute-start | bytes 61448
  283.8 7.8 %collective-permute-start.19 = (f32[80,64]{0,1:T(8,128)S(1)}, f32[80,64]{0,1:T(8,128)S(1)}, u32[]{:S(2)}, u32[]{:S(2)}) collective-permute-start(f32[80,64]{0,1:T(8,128)S(1)} %get-tuple-element.8), channel_id=1, source_target_pairs={{0,96},{16,112},{32,128},{48,144},{64,160},{80,176},{96,192},{112,... | collective-permute-start | bytes 61448
  291.6 1.9 collective-permute-start.20
  293.5 2.5 collective-permute-start.21
  296.0 2.8 collective-permute-start.22
  298.9 1.6 collective-permute-start.23
  300.5 2.8 collective-permute-start.24
  303.4 3.8 %collective-permute-start.25 = (f32[80,64]{0,1:T(8,128)S(1)}, f32[80,64]{0,1:T(8,128)S(1)}, u32[]{:S(2)}, u32[]{:S(2)}) collective-permute-start(f32[80,64]{0,1:T(8,128)S(1)} %get-tuple-element.8), channel_id=1, source_target_pairs={{0,192},{16,208},{32,224},{48,240},{64,256},{80,272},{96,288},{112... | collective-permute-start | bytes 61448
  307.2 1.6 collective-permute-start.26
  308.8 2.5 collective-permute-start
  311.3 2.0 collective-permute-start.1
  313.2 2.9 collective-permute-start.10
  319.4 2.2 collective-permute-start.11
  321.6 2.3 concatenate.1
  323.9 1.8 collective-permute-start.12
  325.7 4.5 %collective-permute-start.2 = (f32[64,64]{0,1:T(8,128)S(1)}, f32[64,64]{0,1:T(8,128)S(1)}, u32[]{:S(2)}, u32[]{:S(2)}) collective-permute-start(f32[64,64]{0,1:T(8,128)S(1)} %get-tuple-element.7), channel_id=1, source_target_pairs={{0,48},{16,64},{32,80},{48,96},{64,112},{80,128},{96,144},{112,160... | collective-permute-start | bytes 49160
  330.2 2.5 collective-permute-start.3
  335.1 9.7 %all-to-all-start.1 = ((f32[16,1,250]{2,1,0:T(1,128)}), f32[16,1,250]{2,1,0:T(1,128)S(1)}, u32[]{:S(2)}, u32[]{:S(2)}) async-start(f32[16,1,250]{2,1,0:T(1,128)} %reshape.47), calls=%async_computation.1 | async-start | bytes 32768 | tf_op jit(solution)/shard_map/all_to_all | solution.py:80
  344.7 2.6 collective-permute-start.5
  347.4 3.4 collective-permute-start.6
  350.8 2.4 collective-permute-start.7
  353.2 1.7 collective-permute-start.8
  354.9 1.6 collective-permute-start.9
  357.5 2.3 concatenate
  (85 shorter events, 20.1 us)
Async XLA Ops:
  0.0 113.5 %copy-start = (bf16[1,144,3200]{2,1,0:T(8,128)(2,1)S(1)}, bf16[1,144,3200]{2,1,0:T(8,128)(2,1)}, u32[]{:S(2)}) copy-start(bf16[1,144,3200]{2,1,0:T(8,128)(2,1)} %param.22) | copy-start | bytes 2764804
  64.3 46.5 %all-to-all-start = ((bf16[16,5,3200]{2,1,0:T(8,128)(2,1)}), bf16[16,5,3200]{2,1,0:T(8,128)(2,1)S(1)}, u32[]{:S(2)}, u32[]{:S(2)}) async-start(bf16[16,5,3200]{2,1,0:T(8,128)(2,1)} %reshape.27), calls=%async_computation | async-start | bytes 1638400 | tf_op jit(solution)/shard_map/all_to_all | solution.py:57
  77.7 35.9 %copy-start.4 = (bf16[1,80,144]{1,2,0:T(8,128)(2,1)S(1)}, bf16[1,80,144]{1,2,0:T(8,128)(2,1)}, u32[]{:S(2)}) copy-start(bf16[1,80,144]{1,2,0:T(8,128)(2,1)} %param.20) | copy-start | bytes 69124
  266.5 17.3 %collective-permute-start.14 = (f32[80,64]{0,1:T(8,128)S(1)}, f32[80,64]{0,1:T(8,128)S(1)}, u32[]{:S(2)}, u32[]{:S(2)}) collective-permute-start(f32[80,64]{0,1:T(8,128)S(1)} %get-tuple-element.8), channel_id=1, source_target_pairs={{0,16},{16,32},{32,48},{48,64},{64,80},{80,96},{96,112},{112,128},... | collective-permute-start | bytes 61448
  268.4 23.2 %collective-permute-start.15 = (f32[80,64]{0,1:T(8,128)S(1)}, f32[80,64]{0,1:T(8,128)S(1)}, u32[]{:S(2)}, u32[]{:S(2)}) collective-permute-start(f32[80,64]{0,1:T(8,128)S(1)} %get-tuple-element.8), channel_id=1, source_target_pairs={{0,32},{16,48},{32,64},{48,80},{64,96},{80,112},{96,128},{112,144}... | collective-permute-start | bytes 61448
  269.8 3.9 %collective-permute-start.27 = (f32[80,50]{0,1:T(8,128)S(1)}, f32[80,50]{0,1:T(8,128)S(1)}, u32[]{:S(2)}, u32[]{:S(2)}) collective-permute-start(f32[80,50]{0,1:T(8,128)S(1)} %slice.3), channel_id=1, source_target_pairs={{0,224},{16,240},{32,256},{48,272},{64,288},{80,304},{96,320},{112... | collective-permute-start | bytes 48008
  271.0 22.5 %collective-permute-start.16 = (f32[80,64]{0,1:T(8,128)S(1)}, f32[80,64]{0,1:T(8,128)S(1)}, u32[]{:S(2)}, u32[]{:S(2)}) collective-permute-start(f32[80,64]{0,1:T(8,128)S(1)} %get-tuple-element.8), channel_id=1, source_target_pairs={{0,48},{16,64},{32,80},{48,96},{64,112},{80,128},{96,144},{112,160... | collective-permute-start | bytes 61448
  272.3 23.7 %collective-permute-start.17 = (f32[80,64]{0,1:T(8,128)S(1)}, f32[80,64]{0,1:T(8,128)S(1)}, u32[]{:S(2)}, u32[]{:S(2)}) collective-permute-start(f32[80,64]{0,1:T(8,128)S(1)} %get-tuple-element.8), channel_id=1, source_target_pairs={{0,64},{16,80},{32,96},{48,112},{64,128},{80,144},{96,160},{112,17... | collective-permute-start | bytes 61448
  273.7 25.2 %collective-permute-start.18 = (f32[80,64]{0,1:T(8,128)S(1)}, f32[80,64]{0,1:T(8,128)S(1)}, u32[]{:S(2)}, u32[]{:S(2)}) collective-permute-start(f32[80,64]{0,1:T(8,128)S(1)} %get-tuple-element.8), channel_id=1, source_target_pairs={{0,80},{16,96},{32,112},{48,128},{64,144},{80,160},{96,176},{112,1... | collective-permute-start | bytes 61448
  283.8 16.7 %collective-permute-start.19 = (f32[80,64]{0,1:T(8,128)S(1)}, f32[80,64]{0,1:T(8,128)S(1)}, u32[]{:S(2)}, u32[]{:S(2)}) collective-permute-start(f32[80,64]{0,1:T(8,128)S(1)} %get-tuple-element.8), channel_id=1, source_target_pairs={{0,96},{16,112},{32,128},{48,144},{64,160},{80,176},{96,192},{112,... | collective-permute-start | bytes 61448
  291.6 11.8 %collective-permute-start.20 = (f32[80,64]{0,1:T(8,128)S(1)}, f32[80,64]{0,1:T(8,128)S(1)}, u32[]{:S(2)}, u32[]{:S(2)}) collective-permute-start(f32[80,64]{0,1:T(8,128)S(1)} %get-tuple-element.8), channel_id=1, source_target_pairs={{0,112},{16,128},{32,144},{48,160},{64,176},{80,192},{96,208},{112... | collective-permute-start | bytes 61448
  293.5 13.6 %collective-permute-start.21 = (f32[80,64]{0,1:T(8,128)S(1)}, f32[80,64]{0,1:T(8,128)S(1)}, u32[]{:S(2)}, u32[]{:S(2)}) collective-permute-start(f32[80,64]{0,1:T(8,128)S(1)} %get-tuple-element.8), channel_id=1, source_target_pairs={{0,128},{16,144},{32,160},{48,176},{64,192},{80,208},{96,224},{112... | collective-permute-start | bytes 61448
  296.0 12.7 %collective-permute-start.22 = (f32[80,64]{0,1:T(8,128)S(1)}, f32[80,64]{0,1:T(8,128)S(1)}, u32[]{:S(2)}, u32[]{:S(2)}) collective-permute-start(f32[80,64]{0,1:T(8,128)S(1)} %get-tuple-element.8), channel_id=1, source_target_pairs={{0,144},{16,160},{32,176},{48,192},{64,208},{80,224},{96,240},{112... | collective-permute-start | bytes 61448
  298.9 12.4 %collective-permute-start.23 = (f32[80,64]{0,1:T(8,128)S(1)}, f32[80,64]{0,1:T(8,128)S(1)}, u32[]{:S(2)}, u32[]{:S(2)}) collective-permute-start(f32[80,64]{0,1:T(8,128)S(1)} %get-tuple-element.8), channel_id=1, source_target_pairs={{0,160},{16,176},{32,192},{48,208},{64,224},{80,240},{96,256},{112... | collective-permute-start | bytes 61448
  300.5 12.7 %collective-permute-start.24 = (f32[80,64]{0,1:T(8,128)S(1)}, f32[80,64]{0,1:T(8,128)S(1)}, u32[]{:S(2)}, u32[]{:S(2)}) collective-permute-start(f32[80,64]{0,1:T(8,128)S(1)} %get-tuple-element.8), channel_id=1, source_target_pairs={{0,176},{16,192},{32,208},{48,224},{64,240},{80,256},{96,272},{112... | collective-permute-start | bytes 61448
  303.4 12.7 %collective-permute-start.25 = (f32[80,64]{0,1:T(8,128)S(1)}, f32[80,64]{0,1:T(8,128)S(1)}, u32[]{:S(2)}, u32[]{:S(2)}) collective-permute-start(f32[80,64]{0,1:T(8,128)S(1)} %get-tuple-element.8), channel_id=1, source_target_pairs={{0,192},{16,208},{32,224},{48,240},{64,256},{80,272},{96,288},{112... | collective-permute-start | bytes 61448
  307.2 12.2 %collective-permute-start.26 = (f32[80,64]{0,1:T(8,128)S(1)}, f32[80,64]{0,1:T(8,128)S(1)}, u32[]{:S(2)}, u32[]{:S(2)}) collective-permute-start(f32[80,64]{0,1:T(8,128)S(1)} %get-tuple-element.8), channel_id=1, source_target_pairs={{0,208},{16,224},{32,240},{48,256},{64,272},{80,288},{96,304},{112... | collective-permute-start | bytes 61448
  308.8 16.9 %collective-permute-start = (f32[64,64]{0,1:T(8,128)S(1)}, f32[64,64]{0,1:T(8,128)S(1)}, u32[]{:S(2)}, u32[]{:S(2)}) collective-permute-start(f32[64,64]{0,1:T(8,128)S(1)} %get-tuple-element.7), channel_id=1, source_target_pairs={{0,16},{16,32},{32,48},{48,64},{64,80},{80,96},{96,112},{112,128},... | collective-permute-start | bytes 49160
  311.3 18.9 %collective-permute-start.1 = (f32[64,64]{0,1:T(8,128)S(1)}, f32[64,64]{0,1:T(8,128)S(1)}, u32[]{:S(2)}, u32[]{:S(2)}) collective-permute-start(f32[64,64]{0,1:T(8,128)S(1)} %get-tuple-element.7), channel_id=1, source_target_pairs={{0,32},{16,48},{32,64},{48,80},{64,96},{80,112},{96,128},{112,144}... | collective-permute-start | bytes 49160
  313.2 19.4 %collective-permute-start.10 = (f32[64,64]{0,1:T(8,128)S(1)}, f32[64,64]{0,1:T(8,128)S(1)}, u32[]{:S(2)}, u32[]{:S(2)}) collective-permute-start(f32[64,64]{0,1:T(8,128)S(1)} %get-tuple-element.7), channel_id=1, source_target_pairs={{0,176},{16,192},{32,208},{48,224},{64,240},{80,256},{96,272},{112... | collective-permute-start | bytes 49160
  316.1 7.7 %collective-permute-start.13 = (f32[64,50]{0,1:T(8,128)S(1)}, f32[64,50]{0,1:T(8,128)S(1)}, u32[]{:S(2)}, u32[]{:S(2)}) collective-permute-start(f32[64,50]{0,1:T(8,128)S(1)} %slice.2), channel_id=1, source_target_pairs={{0,224},{16,240},{32,256},{48,272},{64,288},{80,304},{96,320},{112... | collective-permute-start | bytes 38408
  319.4 25.3 %collective-permute-start.11 = (f32[64,64]{0,1:T(8,128)S(1)}, f32[64,64]{0,1:T(8,128)S(1)}, u32[]{:S(2)}, u32[]{:S(2)}) collective-permute-start(f32[64,64]{0,1:T(8,128)S(1)} %get-tuple-element.7), channel_id=1, source_target_pairs={{0,192},{16,208},{32,224},{48,240},{64,256},{80,272},{96,288},{112... | collective-permute-start | bytes 49160
  323.9 23.5 %collective-permute-start.12 = (f32[64,64]{0,1:T(8,128)S(1)}, f32[64,64]{0,1:T(8,128)S(1)}, u32[]{:S(2)}, u32[]{:S(2)}) collective-permute-start(f32[64,64]{0,1:T(8,128)S(1)} %get-tuple-element.7), channel_id=1, source_target_pairs={{0,208},{16,224},{32,240},{48,256},{64,272},{80,288},{96,304},{112... | collective-permute-start | bytes 49160
  325.7 25.1 %collective-permute-start.2 = (f32[64,64]{0,1:T(8,128)S(1)}, f32[64,64]{0,1:T(8,128)S(1)}, u32[]{:S(2)}, u32[]{:S(2)}) collective-permute-start(f32[64,64]{0,1:T(8,128)S(1)} %get-tuple-element.7), channel_id=1, source_target_pairs={{0,48},{16,64},{32,80},{48,96},{64,112},{80,128},{96,144},{112,160... | collective-permute-start | bytes 49160
  330.2 23.0 %collective-permute-start.3 = (f32[64,64]{0,1:T(8,128)S(1)}, f32[64,64]{0,1:T(8,128)S(1)}, u32[]{:S(2)}, u32[]{:S(2)}) collective-permute-start(f32[64,64]{0,1:T(8,128)S(1)} %get-tuple-element.7), channel_id=1, source_target_pairs={{0,64},{16,80},{32,96},{48,112},{64,128},{80,144},{96,160},{112,17... | collective-permute-start | bytes 49160
  332.7 22.2 %collective-permute-start.4 = (f32[64,64]{0,1:T(8,128)S(1)}, f32[64,64]{0,1:T(8,128)S(1)}, u32[]{:S(2)}, u32[]{:S(2)}) collective-permute-start(f32[64,64]{0,1:T(8,128)S(1)} %get-tuple-element.7), channel_id=1, source_target_pairs={{0,80},{16,96},{32,112},{48,128},{64,144},{80,160},{96,176},{112,1... | collective-permute-start | bytes 49160
  335.1 24.8 %all-to-all-start.1 = ((f32[16,1,250]{2,1,0:T(1,128)}), f32[16,1,250]{2,1,0:T(1,128)S(1)}, u32[]{:S(2)}, u32[]{:S(2)}) async-start(f32[16,1,250]{2,1,0:T(1,128)} %reshape.47), calls=%async_computation.1 | async-start | bytes 32768 | tf_op jit(solution)/shard_map/all_to_all | solution.py:80
  344.7 11.8 %collective-permute-start.5 = (f32[64,64]{0,1:T(8,128)S(1)}, f32[64,64]{0,1:T(8,128)S(1)}, u32[]{:S(2)}, u32[]{:S(2)}) collective-permute-start(f32[64,64]{0,1:T(8,128)S(1)} %get-tuple-element.7), channel_id=1, source_target_pairs={{0,96},{16,112},{32,128},{48,144},{64,160},{80,176},{96,192},{112,... | collective-permute-start | bytes 49160
  347.4 9.2 %collective-permute-start.6 = (f32[64,64]{0,1:T(8,128)S(1)}, f32[64,64]{0,1:T(8,128)S(1)}, u32[]{:S(2)}, u32[]{:S(2)}) collective-permute-start(f32[64,64]{0,1:T(8,128)S(1)} %get-tuple-element.7), channel_id=1, source_target_pairs={{0,112},{16,128},{32,144},{48,160},{64,176},{80,192},{96,208},{112... | collective-permute-start | bytes 49160
  350.8 5.8 %collective-permute-start.7 = (f32[64,64]{0,1:T(8,128)S(1)}, f32[64,64]{0,1:T(8,128)S(1)}, u32[]{:S(2)}, u32[]{:S(2)}) collective-permute-start(f32[64,64]{0,1:T(8,128)S(1)} %get-tuple-element.7), channel_id=1, source_target_pairs={{0,128},{16,144},{32,160},{48,176},{64,192},{80,208},{96,224},{112... | collective-permute-start | bytes 49160
  353.2 3.4 collective-permute-start.8
  354.9 2.7 collective-permute-start.9
  (10 other events, 66.0 us)
where the time goes:
time: 366 us; the launch traced here: 362 us
  blocking collectives  212 us (58%)
  starting transfers between devices  94.1 us (26%)
  waiting for transfers between devices  34.1 us (9%)
  local copies, waits for them, and re-layouts  11.6 us (3%)
  matrix products  8.14 us (2%)
    unnamed x1, blocking collectives  150 us
    unnamed x28, starting transfers between devices  74.8 us
    all_gather x1, blocking collectives, body(): full_rows = lax.all_gather(grad_out, 'dp', axis=1, tiled=True)  61.9 us
    all_to_all x1, waiting for transfers between devices, body(): lax.all_to_all(sent_rows.reshape(expert_count, slot_count, full_rows.shap...  33.1 us
    all_to_all x1, starting transfers between devices, body(): lax.all_to_all(routed_cols.reshape(expert_count, slot_count, routed_cols....  9.66 us
    all_to_all x1, starting transfers between devices, body(): lax.all_to_all(sent_rows.reshape(expert_count, slot_count, full_rows.shap...  9.65 us
    unnamed x34, local copies, waits for them, and re-layouts  8.19 us
  transfers between devices with their start and end apart: 30, of which 2 were waited for; matrix products, arithmetic and copies ran while one was open for 3% of the time, Pallas kernels for 0%

commit v1 on v0

v1 whole, which is shorter than its diff:
```python
import jax
import jax.numpy as jnp
from jax import lax
from jax.experimental import pallas as pl
from jax.experimental.pallas import tpu as pltpu
from jax.sharding import PartitionSpec as P

BF = jnp.bfloat16
F32 = jnp.float32
MESH = pl.DeviceIdType.MESH
NX, NY, NZ = 4, 8, 16
CHIPS = NX * NY
TOK = 64
CAP = 5
ROUTED = NZ * CAP
HID = 144
FEAT = 50
CHUNK = 2 * FEAT
LANES = 128
WIDTH = CHIPS * CHUNK
NEAR_FIRST = (1, 7, 2, 6, 3, 5, 4)
FAR_FIRST = (4, 3, 5, 2, 6, 1, 7, 0)
X_STEPS = (2, 1, 3)


def nt_dot(a, b):
    return lax.dot_general(a, b, (((1,), (1,)), ((), ())), preferred_element_type=F32)


def nn_dot(a, b):
    return lax.dot_general(a, b, (((1,), (0,)), ((), ())), preferred_element_type=F32)


def silu_grads(grad_hidden, gate_pre, up_pre):
    g = gate_pre.astype(F32)
    u = up_pre.astype(F32)
    s = 1.0 / (1.0 + jnp.exp(-g))
    dgate = grad_hidden * u * s * (1.0 + g * (1.0 - s))
    dup = grad_hidden * g * s
    return dgate.astype(BF), dup.astype(BF)


def kernel(
    x_hbm, eidx_hbm, slot_hbm, cap_hbm, share_hbm,
    rg_hbm, ru_hbm, gw_hbm, uw_hbm, dw_hbm,
    sg_hbm, su_hbm, gc_hbm, uc_hbm, dc_hbm,
    out_ref,
    x_mine, x_other, eidx, slot, cap, share,
    pre_rg, pre_ru, pre_sg, pre_su,
    raw, win, place,
    z_out, z_in, z2_out, z2_in, slots,
    rows_r, rows_s,
    part_out, part_in, four, own, sums, x_in, y_out, y_in,
    shared_sum, total,
    in_sem, pair_snd, pair_rcv, z_snd, z_rcv, z2_snd, z2_rcv,
    gy_snd, gy_rcv, gx_snd, gx_rcv, gs_snd, gs_rcv,
    p_snd, p_rcv, rx_snd, rx_rcv, ry_snd, ry_rcv,
):
    dp = lax.axis_index("dp")
    z = lax.axis_index("expert")
    core = lax.rem(dp, 2)
    chip = dp // 2
    x = lax.rem(chip, NX)
    y = chip // NX

    def at_y(k):
        yy = lax.rem(y + k, NY)
        return yy, ((yy * NX + x) * 2 + core, z)

    def at_x(k):
        xx = lax.rem(x + k, NX)
        return xx, ((y * NX + xx) * 2 + core, z)

    def at_z(k):
        zz = lax.rem(z + k, NZ)
        return zz, (dp, zz)

    sibling = (chip * 2 + 1 - core, z)

    def remote(src, dst, snd, rcv, dev):
        return pltpu.make_async_remote_copy(
            src_ref=src, dst_ref=dst, send_sem=snd, recv_sem=rcv, device_id=dev, device_id_type=MESH
        )

    barrier = pltpu.get_barrier_semaphore()
    pl.semaphore_signal(barrier, inc=1, device_id=sibling, device_id_type=MESH)
    for k in NEAR_FIRST:
        pl.semaphore_signal(barrier, inc=1, device_id=at_y(k)[1], device_id_type=MESH)
    for k in X_STEPS:
        pl.semaphore_signal(barrier, inc=1, device_id=at_x(k)[1], device_id_type=MESH)

    @pl.when(core == 0)
    def _():
        for k in range(1, NZ):
            pl.semaphore_signal(barrier, inc=1, device_id=at_z(k)[1], device_id_type=MESH)

    small = (
        (x_hbm, x_mine), (eidx_hbm, eidx), (slot_hbm, slot), (cap_hbm, cap), (share_hbm, share),
        (rg_hbm.at[0], pre_rg), (ru_hbm.at[0], pre_ru), (sg_hbm, pre_sg), (su_hbm, pre_su),
    )
    weights = (dc_hbm, gc_hbm, uc_hbm, dw_hbm.at[0], gw_hbm.at[0], uw_hbm.at[0])
    loads = [pltpu.make_async_copy(s, d, in_sem.at[i]) for i, (s, d) in enumerate(small)]
    for i, w in enumerate(weights):
        loads.append(pltpu.make_async_copy(w, raw.at[i, :, pl.ds(0, WIDTH)], in_sem.at[len(small) + i]))
    for c in loads:
        c.start()
    for i in range(6):
        raw[i, :, WIDTH:] = jnp.zeros((HID, LANES), BF)
    for c in loads[: len(small)]:
        c.wait()

    @pl.when(core == 0)
    def _():
        pl.semaphore_wait(barrier, 1 + NY - 1 + NX - 1 + NZ - 1)

    @pl.when(core == 1)
    def _():
        pl.semaphore_wait(barrier, 1 + NY - 1 + NX - 1)

    pair = remote(x_mine, x_other, pair_snd.at[0], pair_rcv.at[0], sibling)
    pair.start()

    def window(i):
        loads[len(small) + i].wait()
        for c in range(CHIPS):
            q, o = divmod(c * CHUNK, LANES)
            wide = raw[i, :, q * LANES : (q + 2) * LANES] if o else None
            piece = raw[i, :, q * LANES : (q + 1) * LANES] if o == 0 else wide[:, o : o + LANES]
            win[i, c // NX, :, (c % NX) * LANES : (c % NX + 1) * LANES] = piece

    lane = lax.broadcasted_iota(jnp.int32, (FEAT, LANES), 1)
    feat = lax.broadcasted_iota(jnp.int32, (FEAT, LANES), 0)
    put_mine = (lane == feat + FEAT * core).astype(BF)
    put_other = (lane == feat + FEAT * (1 - core)).astype(BF)

    def chip_rows():
        pair.wait()
        return (nn_dot(x_mine[...], put_mine) + nn_dot(x_other[...], put_other)).astype(BF)

    def send_y(rows):
        for k in NEAR_FIRST:
            remote(rows.at[y, x], rows.at[y, x], gy_snd.at[k], gy_rcv.at[k], at_y(k)[1]).start()

    def send_x(rows, k, yy):
        for j in X_STEPS:
            i = k * NX + j
            remote(rows.at[yy, x], rows.at[yy, x], gx_snd.at[i], gx_rcv.at[i], at_x(j)[1]).start()

    def relay_x(rows):
        send_x(rows, 0, y)
        for k in NEAR_FIRST:
            yy = lax.rem(y - k + NY, NY)
            remote(rows.at[yy, x], rows.at[yy, x], gy_snd.at[k], gy_rcv.at[k], at_y(k)[1]).wait_recv()
            send_x(rows, k, yy)

    def share_row(rows, k):
        yy = lax.rem(y - k + NY, NY)
        for j in X_STEPS:
            i = k * NX + j
            xx = lax.rem(x - j + NX, NX)
            remote(rows.at[yy, xx], rows.at[yy, xx], gx_snd.at[i], gx_rcv.at[i], at_x(j)[1]).wait_recv()
        remote(rows.at[yy], rows.at[yy], gs_snd.at[k], gs_rcv.at[k], sibling).start()
        return yy

    def take_row(rows, k):
        yy = lax.rem(y - k + NY, NY)
        remote(rows.at[yy], rows.at[yy], gs_snd.at[k], gs_rcv.at[k], sibling).wait_recv()
        return yy

    def hidden(rows, down, get_row):
        acc = None
        for k in (0,) + NEAR_FIRST:
            yy = get_row(rows, k)
            wide = jnp.concatenate([rows[yy, j] for j in range(NX)], axis=1)
            term = nt_dot(wide, win[down, yy])
            acc = term if acc is None else acc + term
        return acc

    def send_part(n, dg, du, gate, up):
        for k in FAR_FIRST:
            yy = lax.rem(y + k, NY)
            t = nn_dot(dg, win[gate, yy]) + nn_dot(du, win[up, yy])
            for j in range(NX):
                part_out[yy, j, 0:n] = t[:, j * LANES : (j + 1) * LANES].astype(BF)
            ref_out, ref_in = part_out.at[yy, :, pl.ds(0, n)], part_in.at[yy, :, pl.ds(0, n)]
            remote(ref_out, ref_in, p_snd.at[k], p_rcv.at[k], sibling).start()

    def own_part(n, dg, du, gate, up):
        for k in FAR_FIRST:
            yy = lax.rem(y + k, NY)
            t = nn_dot(dg, win[gate, yy]) + nn_dot(du, win[up, yy])
            ref_out, ref_in = part_out.at[yy, :, pl.ds(0, n)], part_in.at[yy, :, pl.ds(0, n)]
            remote(ref_out, ref_in, p_snd.at[k], p_rcv.at[k], sibling).wait_recv()
            for j in range(NX):
                s = t[:, j * LANES : (j + 1) * LANES] + part_in[yy, j, 0:n].astype(F32)
                four[j, 0:n] = s
                sums[yy, j, 0:n] = s.astype(BF)
            own[yy, 0:n] = four[x, 0:n]
            for j in X_STEPS:
                xx, dev = at_x(j)
                i = k * NX + j
                remote(
                    sums.at[yy, xx, pl.ds(0, n)], x_in.at[yy, j, pl.ds(0, n)],
                    rx_snd.at[i], rx_rcv.at[i], dev,
                ).start()

    def add_x(n, k):
        yy = lax.rem(y + k, NY)
        acc = own[yy, 0:n]
        for j in X_STEPS:
            i = k * NX + j
            remote(
                sums.at[yy, j, pl.ds(0, n)], x_in.at[yy, j, pl.ds(0, n)],
                rx_snd.at[i], rx_rcv.at[i], at_x(j)[1],
            ).wait_recv()
            acc += x_in[yy, j, 0:n].astype(F32)
        return acc

    def reduce(n):
        for k in FAR_FIRST[:-1]:
            y_out[k, 0:n] = add_x(n, k).astype(BF)
            remote(
                y_out.at[k, pl.ds(0, n)], y_in.at[k, pl.ds(0, n)], ry_snd.at[k], ry_rcv.at[k], at_y(k)[1]
            ).start()
        acc = add_x(n, 0)
        for k in NEAR_FIRST:
            remote(
                y_out.at[k, pl.ds(0, n)], y_in.at[k, pl.ds(0, n)], ry_snd.at[k], ry_rcv.at[k], at_y(k)[1]
            ).wait_recv()
            acc += y_in[k, 0:n].astype(F32)
        return acc

    def wait_sends(rows, n, other_n):
        for k in NEAR_FIRST:
            remote(rows.at[y, x], rows.at[y, x], gy_snd.at[k], gy_rcv.at[k], at_y(k)[1]).wait_send()
            remote(
                y_out.at[k, pl.ds(0, n)], y_in.at[k, pl.ds(0, n)], ry_snd.at[k], ry_rcv.at[k], at_y(k)[1]
            ).wait_send()
        for k in range(NY):
            remote(rows.at[y], rows.at[y], gs_snd.at[k], gs_rcv.at[k], sibling).wait_send()
            ref_out = part_out.at[k, :, pl.ds(0, other_n)]
            ref_in = part_in.at[k, :, pl.ds(0, other_n)]
            remote(ref_out, ref_in, p_snd.at[k], p_rcv.at[k], sibling).wait_send()
            for j in X_STEPS:
                i = k * NX + j
                remote(rows.at[y, x], rows.at[y, x], gx_snd.at[i], gx_rcv.at[i], at_x(j)[1]).wait_send()
                remote(
                    sums.at[k, j, pl.ds(0, n)], x_in.at[k, j, pl.ds(0, n)],
                    rx_snd.at[i], rx_rcv.at[i], at_x(j)[1],
                ).wait_send()

    answer = remote(shared_sum.at[0], shared_sum.at[1], pair_snd.at[1], pair_rcv.at[1], sibling)
    result = remote(total.at[0], total.at[1], pair_snd.at[2], pair_rcv.at[2], sibling)

    @pl.when(core == 0)
    def _():
        expert_row = eidx[...]
        token_cap = jnp.zeros((1, TOK), jnp.int32)
        for e in range(NZ):
            token_cap = jnp.where(expert_row == e, cap[:, e : e + 1], token_cap)
        target = expert_row * 8 + slot[...]
        row_ids = lax.broadcasted_iota(jnp.int32, (NZ * 8, TOK), 0)
        placing = ((row_ids == target) & (slot[...] < token_cap)).astype(F32)
        place[...] = placing.T
        eye = lax.broadcasted_iota(jnp.int32, (TOK, TOK), 0) == lax.broadcasted_iota(jnp.int32, (TOK, TOK), 1)
        share_col = jnp.sum(jnp.where(eye, share[...], 0.0), axis=1, keepdims=True)
        z2_out[...] = jnp.zeros_like(z2_out)
        scaled = (share_col * chip_rows().astype(F32)).astype(BF)
        z_out[...] = nn_dot(placing.astype(BF), scaled).reshape(NZ, 8, LANES)
        for k in range(1, NZ):
            zz, dev = at_z(k)
            remote(z_out.at[zz], z_in.at[z], z_snd.at[k], z_rcv.at[k], dev).start()
        z_in[z] = z_out[z]
        window(0)
        window(1)
        window(2)
        for k in range(1, NZ):
            zz = lax.rem(z - k + NZ, NZ)
            remote(z_out.at[zz], z_in.at[zz], z_snd.at[k], z_rcv.at[k], at_z(k)[1]).wait_recv()
        for b in range(NZ):
            slots[b * CAP : (b + 1) * CAP] = z_in[b, 0:CAP]
        rows_r[y, x] = slots[...].astype(BF)
        send_y(rows_r)
        window(3)
        relay_x(rows_r)
        dg, du = silu_grads(hidden(rows_s, 0, take_row), pre_sg[...], pre_su[...])
        send_part(TOK, dg, du, 1, 2)
        window(4)
        window(5)
        dg, du = silu_grads(hidden(rows_r, 3, share_row), pre_rg[...], pre_ru[...])
        own_part(ROUTED, dg, du, 4, 5)
        slots[...] = reduce(ROUTED)
        for b in range(NZ):
            z2_out[b, 0:CAP] = slots[b * CAP : (b + 1) * CAP]
        for k in range(1, NZ):
            zz, dev = at_z(k)
            remote(z2_out.at[zz], z2_in.at[z], z2_snd.at[k], z2_rcv.at[k], dev).start()
        z2_in[z] = z2_out[z]
        wait_sends(rows_r, ROUTED, TOK)
        for k in range(1, NZ):
            zz = lax.rem(z - k + NZ, NZ)
            remote(z2_out.at[zz], z2_in.at[zz], z2_snd.at[k], z2_rcv.at[k], at_z(k)[1]).wait_recv()
        back = z2_in[...].reshape(NZ * 8, LANES)
        picked = lax.dot_general(
            place[...], back, (((1,), (0,)), ((), ())),
            precision=lax.Precision.HIGHEST, preferred_element_type=F32,
        )
        answer.wait_recv()
        both = (shared_sum[1] + picked).astype(BF)
        total[0] = both
        result.start()
        out_ref[...] = both[:, 0:FEAT]
        for k in range(1, NZ):
            zz, dev = at_z(k)
            remote(z_out.at[zz], z_in.at[z], z_snd.at[k], z_rcv.at[k], dev).wait_send()
            remote(z2_out.at[zz], z2_in.at[z], z2_snd.at[k], z2_rcv.at[k], dev).wait_send()
        result.wait_send()

    @pl.when(core == 1)
    def _():
        rows_s[y, x] = chip_rows()
        send_y(rows_s)
        window(0)
        relay_x(rows_s)
        window(1)
        window(2)
        dg, du = silu_grads(hidden(rows_s, 0, share_row), pre_sg[...], pre_su[...])
        window(3)
        window(4)
        window(5)
        own_part(TOK, dg, du, 1, 2)
        dg, du = silu_grads(hidden(rows_r, 3, take_row), pre_rg[...], pre_ru[...])
        send_part(ROUTED, dg, du, 4, 5)
        shared_sum[0] = reduce(TOK)
        answer.start()
        wait_sends(rows_s, TOK, ROUTED)
        answer.wait_send()
        result.wait_recv()
        out_ref[...] = total[1][:, FEAT:CHUNK]


def body(
    grad_out, expert_index, slot_index, capacity, router_share,
    routed_gate, routed_up, gate_weight, up_weight, down_weight,
    shared_gate, shared_up, gate_common, up_common, down_common,
):
    dma = pltpu.SemaphoreType.DMA
    scratch = [
        pltpu.VMEM((TOK, FEAT), BF), pltpu.VMEM((TOK, FEAT), BF),
        pltpu.VMEM((1, TOK), jnp.int32), pltpu.VMEM((1, TOK), jnp.int32),
        pltpu.VMEM((1, NZ), jnp.int32), pltpu.VMEM((1, TOK), F32),
        pltpu.VMEM((ROUTED, HID), BF), pltpu.VMEM((ROUTED, HID), BF),
        pltpu.VMEM((TOK, HID), BF), pltpu.VMEM((TOK, HID), BF),
        pltpu.VMEM((6, HID, WIDTH + LANES), BF),
        pltpu.VMEM((6, NY, HID, NX * LANES), BF),
        pltpu.VMEM((TOK, NZ * 8), F32),
        pltpu.VMEM((NZ, 8, LANES), F32), pltpu.VMEM((NZ, 8, LANES), F32),
        pltpu.VMEM((NZ, 8, LANES), F32), pltpu.VMEM((NZ, 8, LANES), F32),
        pltpu.VMEM((ROUTED, LANES), F32),
        pltpu.VMEM((NY, NX, ROUTED, LANES), BF), pltpu.VMEM((NY, NX, TOK, LANES), BF),
        pltpu.VMEM((NY, NX, ROUTED, LANES), BF), pltpu.VMEM((NY, NX, ROUTED, LANES), BF),
        pltpu.VMEM((NX, ROUTED, LANES), F32), pltpu.VMEM((NY, ROUTED, LANES), F32),
        pltpu.VMEM((NY, NX, ROUTED, LANES), BF), pltpu.VMEM((NY, NX, ROUTED, LANES), BF),
        pltpu.VMEM((NY, ROUTED, LANES), BF), pltpu.VMEM((NY, ROUTED, LANES), BF),
        pltpu.VMEM((2, TOK, LANES), F32), pltpu.VMEM((2, TOK, LANES), BF),
        dma((15,)), dma((3,)), dma((3,)), dma((NZ,)), dma((NZ,)), dma((NZ,)), dma((NZ,)),
        dma((NY,)), dma((NY,)), dma((NY * NX,)), dma((NY * NX,)), dma((NY,)), dma((NY,)),
        dma((NY,)), dma((NY,)), dma((NY * NX,)), dma((NY * NX,)), dma((NY,)), dma((NY,)),
    ]
    return pl.pallas_call(
        kernel,
        out_shape=jax.ShapeDtypeStruct((TOK, FEAT), BF),
        in_specs=[pl.BlockSpec(memory_space=pl.ANY)] * 15,
        out_specs=pl.BlockSpec(memory_space=pltpu.VMEM),
        scratch_shapes=scratch,
        compiler_params=pltpu.CompilerParams(
            collective_id=0, has_side_effects=True, vmem_limit_bytes=56 * 1024 * 1024
        ),
    )(
        grad_out, expert_index.reshape(1, -1), slot_index.reshape(1, -1), capacity.reshape(1, -1),
        router_share.reshape(1, -1), routed_gate, routed_up, gate_weight, up_weight, down_weight,
        shared_gate, shared_up, gate_common, up_common, down_common,
    )


def solution(mesh):
    return jax.shard_map(
        body,
        mesh=mesh,
        in_specs=(
            P("expert", "dp"), P("expert"), P("expert"), P(), P("expert"),
            P("expert", None, "dp"), P("expert", None, "dp"),
            P("expert", "dp", None), P("expert", "dp", None), P("expert", "dp", None),
            P("expert", "dp"), P("expert", "dp"),
            P("dp", None), P("dp", None), P("dp", None),
        ),
        out_specs=P("expert", "dp"),
        check_vma=False,
    )
```

time: 366 us -> 71.9 us (0.20)
  blocking collectives: 212 us -> 0 us
  starting transfers between devices: 94.1 us -> 0 us
  Pallas kernels: 0 us -> 67.2 us
  waiting for transfers between devices: 34.1 us -> 0 us
  matrix products: 8.14 us -> 0 us
  local copies, waits for them, and re-layouts: 11.6 us -> 4.29 us
    unnamed x1 -> x0, blocking collectives: 150 us -> none
    unnamed x28 -> x0, starting transfers between devices: 74.8 us -> none
    pallas_call x0 -> x1, Pallas kernels: none -> 67.2 us  [body(): pl.pallas_call(kernel, out_shape=jax.ShapeDtypeStruct((TOK, FEAT), BF), i...]
    all_gather x1 -> x0, blocking collectives: 61.9 us -> none  [body(): full_rows = lax.all_gather(grad_out, 'dp', axis=1, tiled=True)]
    all_to_all x2 -> x0, waiting for transfers between devices: 33.1 us -> none  [the longest x1 33.1 us: body(): lax.all_to_all(sent_rows.reshape(expert_count, slot_count, full_rows.shap...]
    all_to_all x2 -> x0, starting transfers between devices: 19.3 us -> none  [the longest x1 9.66 us: body(): lax.all_to_all(routed_cols.reshape(expert_count, slot_count, routed_cols....]
    dot_general x7 -> x0, matrix products: 8.14 us -> none  [the longest x2 3.48 us: back_through(): lax.dot_general(grad_rows, down_mat, (((1,), (1,)), ((), ())), preferred_...]
    unnamed x34 -> x7, local copies, waits for them, and re-layouts: 8.19 us -> 2.88 us
  transfers between devices with their start and end apart: 30 -> 0, of which waited for: 2 -> 0; matrix products, arithmetic and copies ran while one was open for 3% -> 0% of each run, Pallas kernels for 0% -> 0%
where the time goes in v1:
time: 71.9 us; the launch traced here: 71.5 us
  Pallas kernels  67.2 us (93%)
  local copies, waits for them, and re-layouts  4.29 us (6%)
    pallas_call x1, Pallas kernels, body(): pl.pallas_call(kernel, out_shape=jax.ShapeDtypeStruct((TOK, FEAT), BF), i...  67.2 us
    unnamed x7, local copies, waits for them, and re-layouts  2.88 us

profile of v1, /device:TPU:1, one launch (start us, length us, event | category | flops | bytes accessed | tf_op | source)
XLA Modules:
  0.0 71.5 jit_solution(10335993456180497856)
XLA Ops:
  0.0 0.0 copy-start
  0.0 1.4 %copy.16.x_hbm = bf16[64,50]{1,0:T(8,128)(2,1)} copy(bf16[64,50]{0,1:T(8,128)(2,1)} %param.15) | data formatting | bytes 12800 | tf_op args[0]
  1.4 0.0 copy-done
  1.4 0.0 copy-start.1
  1.4 0.7 copy.17.rg_hbm
  2.1 0.1 copy-done.1
  2.2 0.7 copy.18.ru_hbm
  2.9 67.2 %shard_map.145 = bf16[64,50]{1,0:T(8,128)(2,1)} custom-call(bf16[64,50]{1,0:T(8,128)(2,1)} %copy.16.x_hbm, s32[1,64]{1,0:T(1,128)} %bitcast.4, s32[1,64]{1,0:T(1,128)} %bitcast.5, s32[1,16]{1,0:T(1,128)} %bitcast.6, f32[1,64]{1,0:T(1,128)} %bitcast.7, bf16[1,80,144]{2,1,0:T(8,128)(2,1)} %copy.17.rg_hbm, bf16[1,80,144]{2,1,0:T(8,128)(2,1)} %copy.18.ru_hbm, ...), custom_call_target="tpu_custom_call" | custom-call | tf_op jit(solution)/shard_map/pallas_call | solution.py:370
  70.1 1.4 %copy.19 = bf16[64,50]{0,1:T(8,128)(2,1)} copy(bf16[64,50]{1,0:T(8,128)(2,1)} %shard_map.145) | data formatting | bytes 12800 | tf_op jit(solution)/shard_map/pallas_call | solution.py:370
Async XLA Ops:
  0.0 1.4 %copy-start = (bf16[1,80,144]{1,2,0:T(8,128)(2,1)S(1)}, bf16[1,80,144]{1,2,0:T(8,128)(2,1)}, u32[]{:S(2)}) copy-start(bf16[1,80,144]{1,2,0:T(8,128)(2,1)} %param.20) | copy-start | bytes 69124
  1.4 0.8 %copy-start.1 = (bf16[1,80,144]{1,2,0:T(8,128)(2,1)S(1)}, bf16[1,80,144]{1,2,0:T(8,128)(2,1)}, u32[]{:S(2)}) copy-start(bf16[1,80,144]{1,2,0:T(8,128)(2,1)} %param.21) | copy-start | bytes 69124

commit v2 on v1

v2 whole, which is shorter than its diff:
```python
import jax
import jax.numpy as jnp
from jax import lax
from jax.experimental import pallas as pl
from jax.experimental.pallas import tpu as pltpu
from jax.sharding import PartitionSpec as P

BF = jnp.bfloat16
F32 = jnp.float32
MESH = pl.DeviceIdType.MESH
NX, NY, NZ = 4, 8, 16
CHIPS = NX * NY
TOK = 64
CAP = 5
ROUTED = NZ * CAP
HID = 144
FEAT = 50
CHUNK = 2 * FEAT
LANES = 128
WIDTH = CHIPS * CHUNK
NEAR_FIRST = (1, 7, 2, 6, 3, 5, 4)
FAR_FIRST = (4, 3, 5, 2, 6, 1, 7, 0)
X_STEPS = (2, 1, 3)
Y_STEPS = (4, 3, 5, 2, 6, 1, 7)
Z_STEPS = (8, 7, 9, 6, 10, 5, 11, 4, 12, 3, 13, 2, 14, 1, 15)


def nt_dot(a, b):
    return lax.dot_general(a, b, (((1,), (1,)), ((), ())), preferred_element_type=F32)


def nn_dot(a, b):
    return lax.dot_general(a, b, (((1,), (0,)), ((), ())), preferred_element_type=F32)


def silu_factors(gate_pre, up_pre):
    g = gate_pre.astype(F32)
    u = up_pre.astype(F32)
    s = 1.0 / (1.0 + jnp.exp(-g))
    return u * s * (1.0 + g * (1.0 - s)), g * s


def kernel(
    x_hbm, eidx_hbm, slot_hbm, cap_hbm, share_hbm,
    rg_hbm, ru_hbm, gw_hbm, uw_hbm, dw_hbm,
    sg_hbm, su_hbm, gc_hbm, uc_hbm, dc_hbm,
    out_ref,
    x_mine, eidx, slot, cap, share,
    pre_r, pre_s, factor_r, factor_s, placed,
    raw, win, place,
    z_out, z_in, z2_out, z2_in, slots,
    rows_r, rows_s,
    four, own, sums, x_in, y_out, y_in,
    shared_sum,
    in_sem, pair_snd, pair_rcv, z_snd, z_rcv, z2_snd, z2_rcv,
    gy_snd, gy_rcv, gx_snd, gx_rcv, swap_snd, swap_rcv, rx_snd, rx_rcv, ry_snd, ry_rcv,
):
    dp = lax.axis_index("dp")
    z = lax.axis_index("expert")
    core = lax.rem(dp, 2)
    chip = dp // 2
    x = lax.rem(chip, NX)
    y = chip // NX

    def at_y(k):
        yy = lax.rem(y + k, NY)
        return yy, ((yy * NX + x) * 2 + core, z)

    def at_x(k):
        xx = lax.rem(x + k, NX)
        return xx, ((y * NX + xx) * 2 + core, z)

    def at_z(k, side):
        zz = lax.rem(z + k, NZ)
        return zz, (chip * 2 + side, zz)

    sibling = (chip * 2 + 1 - core, z)

    def remote(src, dst, snd, rcv, dev):
        return pltpu.make_async_remote_copy(
            src_ref=src, dst_ref=dst, send_sem=snd, recv_sem=rcv, device_id=dev, device_id_type=MESH
        )

    small = ((x_hbm, x_mine), (eidx_hbm, eidx), (slot_hbm, slot), (cap_hbm, cap), (share_hbm, share))
    loads = [pltpu.make_async_copy(s, d, in_sem.at[i]) for i, (s, d) in enumerate(small)]
    routed_in = (dw_hbm.at[0], gw_hbm.at[0], uw_hbm.at[0], rg_hbm.at[0], ru_hbm.at[0])
    shared_in = (dc_hbm, gc_hbm, uc_hbm, sg_hbm, su_hbm)

    def homes(half, pre):
        place_of = [raw.at[half * 3 + i, :, pl.ds(0, WIDTH)] for i in range(3)]
        return place_of + [pre.at[half, i] for i in range(2)]

    def local_loads(sources, pre):
        return [
            pltpu.make_async_copy(s, d, in_sem.at[len(small) + i])
            for i, (s, d) in enumerate(zip(sources, homes(0, pre)))
        ]

    def swaps(sources, pre):
        return [
            remote(s, d, swap_snd.at[i], swap_rcv.at[i], sibling)
            for i, (s, d) in enumerate(zip(sources, homes(1, pre)))
        ]

    def greet(dev):
        pl.semaphore_signal(barrier, inc=1, device_id=dev, device_id_type=MESH)

    barrier = pltpu.get_barrier_semaphore()

    @pl.when(core == 0)
    def _():
        for k in Z_STEPS[:7]:
            greet(at_z(k, 0)[1])
            greet(at_z(k, 1)[1])

    for c in loads:
        c.start()

    @pl.when(core == 0)
    def _():
        for k in Z_STEPS[7:]:
            greet(at_z(k, 0)[1])
            greet(at_z(k, 1)[1])

    for k in Y_STEPS:
        greet(at_y(k)[1])
    for k in X_STEPS:
        greet(at_x(k)[1])
    greet(sibling)

    @pl.when(core == 0)
    def _():
        for c in local_loads(routed_in, pre_r):
            c.start()

    @pl.when(core == 1)
    def _():
        for c in local_loads(shared_in, pre_s):
            c.start()

    for i in range(6):
        raw[i, :, WIDTH:] = jnp.zeros((HID, LANES), BF)
    for c in loads:
        c.wait()

    lane = lax.broadcasted_iota(jnp.int32, (LANES, FEAT), 0)
    feat = lax.broadcasted_iota(jnp.int32, (LANES, FEAT), 1)
    put_mine = (lane == feat + FEAT * core).astype(BF)
    mine = nn_dot(put_mine, x_mine[...]).T
    placed[0] = mine.astype(BF)
    expert_row = eidx[...]
    token_cap = jnp.zeros((1, TOK), jnp.int32)
    for e in range(NZ):
        token_cap = jnp.where(expert_row == e, cap[:, e : e + 1], token_cap)
    target = expert_row * 8 + slot[...]
    row_ids = lax.broadcasted_iota(jnp.int32, (NZ * 8, TOK), 0)
    placing = ((row_ids == target) & (slot[...] < token_cap)).astype(F32)
    eye = lax.broadcasted_iota(jnp.int32, (TOK, TOK), 0) == lax.broadcasted_iota(jnp.int32, (TOK, TOK), 1)
    share_col = jnp.sum(jnp.where(eye, share[...], 0.0), axis=1, keepdims=True)
    scaled = (share_col * mine).astype(BF)
    z_out[...] = nn_dot(placing.astype(BF), scaled).reshape(NZ, 8, LANES)

    pl.semaphore_wait(barrier, 1 + NY - 1 + NX - 1 + NZ - 1)

    pair = remote(placed.at[0], placed.at[1], pair_snd.at[0], pair_rcv.at[0], sibling)

    def send_slots(side):
        for k in Z_STEPS:
            zz, dev = at_z(k, 0)
            i = side * NZ + k
            remote(z_out.at[zz], z_in.at[side, z], z_snd.at[k], z_rcv.at[i], dev).start()

    def wait_slots(side, k):
        zz = lax.rem(z - k + NZ, NZ)
        i = side * NZ + k
        remote(z_out.at[zz], z_in.at[side, zz], z_snd.at[k], z_rcv.at[i], at_z(k, 0)[1]).wait_recv()

    def slots_sent():
        for k in range(1, NZ):
            zz, dev = at_z(k, 0)
            remote(z_out.at[zz], z_in.at[0, z], z_snd.at[k], z_rcv.at[k], dev).wait_send()

    pair_slots = remote(z_out.at[z], z_in.at[1, z], z_snd.at[0], z_rcv.at[NZ], sibling)

    def factors_r():
        g = jnp.concatenate([pre_r[0, 0], pre_r[1, 0]], axis=0)
        u = jnp.concatenate([pre_r[0, 1], pre_r[1, 1]], axis=0)
        a, b = silu_factors(g, u)
        factor_r[0], factor_r[1] = a.T, b.T

    def factors_s():
        for half in range(2):
            a, b = silu_factors(pre_s[half, 0], pre_s[half, 1])
            factor_s[0, :, half * HID : (half + 1) * HID] = a
            factor_s[1, :, half * HID : (half + 1) * HID] = b

    def silu_grads(grad_hidden, factor):
        return (grad_hidden * factor[0]).astype(BF), (grad_hidden * factor[1]).astype(BF)

    def window(i):
        half, kind = divmod(i, 3)
        for c in range(CHIPS):
            q, o = divmod(c * CHUNK, LANES)
            wide = raw[i, :, q * LANES : (q + 2) * LANES] if o else None
            piece = raw[i, :, q * LANES : (q + 1) * LANES] if o == 0 else wide[:, o : o + LANES]
            col = (c % NX) * LANES
            win[kind, c // NX, half * HID : (half + 1) * HID, col : col + LANES] = piece

    def send_y(rows):
        for k in Y_STEPS:
            remote(rows.at[y, x], rows.at[y, x], gy_snd.at[k], gy_rcv.at[k], at_y(k)[1]).start()

    def send_x(rows, k, yy):
        for j in X_STEPS:
            i = k * NX + j
            remote(rows.at[yy, x], rows.at[yy, x], gx_snd.at[i], gx_rcv.at[i], at_x(j)[1]).start()

    def relay_x(rows):
        send_x(rows, 0, y)
        for k in NEAR_FIRST:
            yy = lax.rem(y - k + NY, NY)
            remote(rows.at[yy, x], rows.at[yy, x], gy_snd.at[k], gy_rcv.at[k], at_y(k)[1]).wait_recv()
            send_x(rows, k, yy)

    def row_of(rows, k):
        yy = lax.rem(y - k + NY, NY)
        for j in X_STEPS:
            i = k * NX + j
            xx = lax.rem(x - j + NX, NX)
            remote(rows.at[yy, xx], rows.at[yy, xx], gx_snd.at[i], gx_rcv.at[i], at_x(j)[1]).wait_recv()
        return yy

    def hidden(rows):
        acc = None
        for k in (0,) + NEAR_FIRST:
            yy = row_of(rows, k)
            wide = jnp.concatenate([rows[yy, j] for j in range(NX)], axis=1)
            term = nt_dot(wide, win[0, yy])
            acc = term if acc is None else acc + term
        return acc

    def own_part(n, dg, du):
        for k in FAR_FIRST:
            yy = lax.rem(y + k, NY)
            t = nn_dot(dg, win[1, yy]) + nn_dot(du, win[2, yy])
            for j in range(NX):
                s = t[:, j * LANES : (j + 1) * LANES]
                four[j, 0:n] = s
                sums[yy, j, 0:n] = s.astype(BF)
            own[yy, 0:n] = four[x, 0:n]
            for j in X_STEPS:
                xx, dev = at_x(j)
                i = k * NX + j
                remote(
                    sums.at[yy, xx, pl.ds(0, n)], x_in.at[yy, j, pl.ds(0, n)],
                    rx_snd.at[i], rx_rcv.at[i], dev,
                ).start()

    def add_x(n, k):
        yy = lax.rem(y + k, NY)
        acc = own[yy, 0:n]
        for j in X_STEPS:
            i = k * NX + j
            remote(
                sums.at[yy, j, pl.ds(0, n)], x_in.at[yy, j, pl.ds(0, n)],
                rx_snd.at[i], rx_rcv.at[i], at_x(j)[1],
            ).wait_recv()
            acc += x_in[yy, j, 0:n].astype(F32)
        return acc

    def reduce(n):
        for k in FAR_FIRST[:-1]:
            y_out[k, 0:n] = add_x(n, k).astype(BF)
            remote(
                y_out.at[k, pl.ds(0, n)], y_in.at[k, pl.ds(0, n)], ry_snd.at[k], ry_rcv.at[k], at_y(k)[1]
            ).start()
        acc = add_x(n, 0)
        for k in NEAR_FIRST:
            remote(
                y_out.at[k, pl.ds(0, n)], y_in.at[k, pl.ds(0, n)], ry_snd.at[k], ry_rcv.at[k], at_y(k)[1]
            ).wait_recv()
            acc += y_in[k, 0:n].astype(F32)
        return acc

    def wait_sends(rows, n):
        for k in NEAR_FIRST:
            remote(rows.at[y, x], rows.at[y, x], gy_snd.at[k], gy_rcv.at[k], at_y(k)[1]).wait_send()
            remote(
                y_out.at[k, pl.ds(0, n)], y_in.at[k, pl.ds(0, n)], ry_snd.at[k], ry_rcv.at[k], at_y(k)[1]
            ).wait_send()
        for k in range(NY):
            for j in X_STEPS:
                i = k * NX + j
                remote(rows.at[y, x], rows.at[y, x], gx_snd.at[i], gx_rcv.at[i], at_x(j)[1]).wait_send()
                remote(
                    sums.at[k, j, pl.ds(0, n)], x_in.at[k, j, pl.ds(0, n)],
                    rx_snd.at[i], rx_rcv.at[i], at_x(j)[1],
                ).wait_send()

    answer = remote(shared_sum.at[0], shared_sum.at[1], pair_snd.at[1], pair_rcv.at[1], sibling)
    pair_back = remote(z2_out.at[z], z2_in.at[z], z2_snd.at[NZ], z2_rcv.at[0], sibling)

    def wait_back(k, side):
        zz = lax.rem(z - k + NZ, NZ)
        i = side * NZ + k
        remote(z2_out.at[zz], z2_in.at[zz], z2_snd.at[i], z2_rcv.at[k], at_z(k, side)[1]).wait_recv()

    def token_rows():
        back = z2_in[...].reshape(NZ * 8, LANES)
        return lax.dot_general(
            place[...], back, (((1,), (0,)), ((), ())),
            precision=lax.Precision.HIGHEST, preferred_element_type=F32,
        )

    @pl.when(core == 0)
    def _():
        send_slots(0)
        pair.start()
        for c in swaps(shared_in, pre_s):
            c.start()
        z_in[0, z] = z_out[z]
        place[...] = placing.T
        z2_out[...] = jnp.zeros_like(z2_out)
        loaded = local_loads(routed_in, pre_r)
        for i in range(5):
            loaded[i].wait()
        for i in range(3):
            window(i)
        pair_slots.wait_recv()
        for k in range(1, NZ):
            wait_slots(0, k)
            wait_slots(1, k)
        for b in range(NZ):
            slots[b * CAP : (b + 1) * CAP] = z_in[0, b, 0:CAP] + z_in[1, b, 0:CAP]
        rows_r[y, x] = slots[...].astype(BF)
        send_y(rows_r)
        relay_x(rows_r)
        arrive = swaps(routed_in, pre_r)
        arrive[3].wait_recv()
        arrive[4].wait_recv()
        factors_r()
        for i in range(3):
            arrive[i].wait_recv()
            window(3 + i)
        dg, du = silu_grads(hidden(rows_r), factor_r)
        own_part(ROUTED, dg, du)
        slots[...] = reduce(ROUTED)
        for b in range(NZ):
            z2_out[b, 0:CAP] = slots[b * CAP : (b + 1) * CAP]
        for k in Z_STEPS:
            for side in range(2):
                zz, dev = at_z(k, side)
                i = side * NZ + k
                remote(z2_out.at[zz], z2_in.at[z], z2_snd.at[i], z2_rcv.at[k], dev).start()
        pair_back.start()
        z2_in[z] = z2_out[z]
        wait_sends(rows_r, ROUTED)
        for c in swaps(shared_in, pre_s):
            c.wait_send()
        slots_sent()
        pair.wait_send()
        answer.wait_recv()
        for k in range(1, NZ):
            wait_back(k, 0)
        out_ref[...] = (shared_sum[1] + token_rows()).T[0:FEAT].astype(BF)
        for k in range(1, NZ):
            for side in range(2):
                zz, dev = at_z(k, side)
                i = side * NZ + k
                remote(z2_out.at[zz], z2_in.at[z], z2_snd.at[i], z2_rcv.at[k], dev).wait_send()
        pair_back.wait_send()

    @pl.when(core == 1)
    def _():
        send_slots(1)
        pair_slots.start()
        pair.wait_recv()
        rows_s[y, x] = placed[0] + placed[1]
        send_y(rows_s)
        for c in swaps(routed_in, pre_r):
            c.start()
        place[...] = placing.T
        loaded = local_loads(shared_in, pre_s)
        for i in range(5):
            loaded[i].wait()
        for i in range(3):
            window(i)
        relay_x(rows_s)
        arrive = swaps(shared_in, pre_s)
        arrive[3].wait_recv()
        arrive[4].wait_recv()
        factors_s()
        for i in range(3):
            arrive[i].wait_recv()
            window(3 + i)
        dg, du = silu_grads(hidden(rows_s), factor_s)
        own_part(TOK, dg, du)
        shared_sum[0] = reduce(TOK)
        answer.start()
        wait_sends(rows_s, TOK)
        for c in swaps(routed_in, pre_r):
            c.wait_send()
        slots_sent()
        pair_slots.wait_send()
        answer.wait_send()
        pair_back.wait_recv()
        for k in range(1, NZ):
            wait_back(k, 1)
        out_ref[...] = (shared_sum[0] + token_rows()).T[FEAT:CHUNK].astype(BF)


def body(
    grad_out, expert_index, slot_index, capacity, router_share,
    routed_gate, routed_up, gate_weight, up_weight, down_weight,
    shared_gate, shared_up, gate_common, up_common, down_common,
):
    dma = pltpu.SemaphoreType.DMA
    scratch = [
        pltpu.VMEM((FEAT, TOK), BF),
        pltpu.VMEM((1, TOK), jnp.int32), pltpu.VMEM((1, TOK), jnp.int32),
        pltpu.VMEM((1, NZ), jnp.int32), pltpu.VMEM((1, TOK), F32),
        pltpu.VMEM((2, 2, HID, ROUTED), BF), pltpu.VMEM((2, 2, TOK, HID), BF),
        pltpu.VMEM((2, ROUTED, 2 * HID), F32), pltpu.VMEM((2, TOK, 2 * HID), F32), pltpu.VMEM((2, TOK, LANES), BF),
        pltpu.VMEM((6, HID, WIDTH + LANES), BF),
        pltpu.VMEM((3, NY, 2 * HID, NX * LANES), BF),
        pltpu.VMEM((TOK, NZ * 8), F32),
        pltpu.VMEM((NZ, 8, LANES), F32), pltpu.VMEM((2, NZ, 8, LANES), F32),
        pltpu.VMEM((NZ, 8, LANES), F32), pltpu.VMEM((NZ, 8, LANES), F32),
        pltpu.VMEM((ROUTED, LANES), F32),
        pltpu.VMEM((NY, NX, ROUTED, LANES), BF), pltpu.VMEM((NY, NX, TOK, LANES), BF),
        pltpu.VMEM((NX, ROUTED, LANES), F32), pltpu.VMEM((NY, ROUTED, LANES), F32),
        pltpu.VMEM((NY, NX, ROUTED, LANES), BF), pltpu.VMEM((NY, NX, ROUTED, LANES), BF),
        pltpu.VMEM((NY, ROUTED, LANES), BF), pltpu.VMEM((NY, ROUTED, LANES), BF),
        pltpu.VMEM((2, TOK, LANES), F32),
        dma((10,)), dma((2,)), dma((2,)), dma((NZ,)), dma((2 * NZ,)), dma((2 * NZ,)), dma((NZ,)),
        dma((NY,)), dma((NY,)), dma((NY * NX,)), dma((NY * NX,)), dma((5,)), dma((5,)),
        dma((NY * NX,)), dma((NY * NX,)), dma((NY,)), dma((NY,)),
    ]
    out = pl.pallas_call(
        kernel,
        out_shape=jax.ShapeDtypeStruct((FEAT, TOK), BF),
        in_specs=[pl.BlockSpec(memory_space=pl.ANY)] * 15,
        out_specs=pl.BlockSpec(memory_space=pltpu.VMEM),
        scratch_shapes=scratch,
        compiler_params=pltpu.CompilerParams(
            collective_id=0, has_side_effects=True, vmem_limit_bytes=56 * 1024 * 1024
        ),
    )(
        grad_out.T, expert_index.reshape(1, -1), slot_index.reshape(1, -1), capacity.reshape(1, -1),
        router_share.reshape(1, -1), routed_gate.swapaxes(1, 2), routed_up.swapaxes(1, 2), gate_weight, up_weight, down_weight,
        shared_gate, shared_up, gate_common, up_common, down_common,
    )
    return out.T


def solution(mesh):
    return jax.shard_map(
        body,
        mesh=mesh,
        in_specs=(
            P("expert", "dp"), P("expert"), P("expert"), P(), P("expert"),
            P("expert", None, "dp"), P("expert", None, "dp"),
            P("expert", "dp", None), P("expert", "dp", None), P("expert", "dp", None),
            P("expert", "dp"), P("expert", "dp"),
            P("dp", None), P("dp", None), P("dp", None),
        ),
        out_specs=P("expert", "dp"),
        check_vma=False,
    )
```

time: 71.9 us -> 64.8 us (0.901)
  Pallas kernels: 67.2 us -> 63.2 us
  local copies, waits for them, and re-layouts: 4.29 us -> 1.31 us
    pallas_call x1, Pallas kernels: 67.2 us -> 63.2 us  [body(): pl.pallas_call(kernel, out_shape=jax.ShapeDtypeStruct((FEAT, TOK), BF), i...]
    unnamed x7 -> x1, local copies, waits for them, and re-layouts: 2.88 us -> 1.31 us
    pallas_call x1 -> x0, local copies, waits for them, and re-layouts: 1.41 us -> none  [body(): pl.pallas_call(kernel, out_shape=jax.ShapeDtypeStruct((TOK, FEAT), BF), i...]
where the time goes in v2:
time: 64.8 us; the launch traced here: 64.5 us
  Pallas kernels  63.2 us (98%)
  local copies, waits for them, and re-layouts  1.31 us (2%)
    pallas_call x1, Pallas kernels, body(): pl.pallas_call(kernel, out_shape=jax.ShapeDtypeStruct((FEAT, TOK), BF), i...  63.2 us
    unnamed x1, local copies, waits for them, and re-layouts  1.31 us

profile of v2, /device:TPU:1, one launch (start us, length us, event | category | flops | bytes accessed | tf_op | source)
XLA Modules:
  0.0 64.5 jit_solution(2030142298176111118)
XLA Ops:
  0.0 63.2 %shard_map.145 = bf16[50,64]{1,0:T(8,128)(2,1)} custom-call(bf16[50,64]{1,0:T(8,128)(2,1)} %bitcast.11, s32[1,64]{1,0:T(1,128)} %bitcast.12, s32[1,64]{1,0:T(1,128)} %bitcast.13, s32[1,16]{1,0:T(1,128)} %bitcast.14, f32[1,64]{1,0:T(1,128)} %bitcast.15, bf16[1,144,80]{2,1,0:T(8,128)(2,1)} %bitcast.9, bf16[1,144,80]{2,1,0:T(8,128)(2,1)} %bitcast.10, ...), custom_call_target="tpu_custom_call" | custom-call | tf_op jit(solution)/shard_map/pallas_call | solution.py:439
  63.2 1.3 %copy.17 = bf16[64,50]{0,1:T(8,128)(2,1)} copy(bf16[64,50]{0,1:T(8,128)(2,1)} %bitcast.8) | data formatting | bytes 12800

commit v3 on v2

--- a/solution.py
+++ b/solution.py
@@ -107,25 +107,31 @@
 
     barrier = pltpu.get_barrier_semaphore()
 
-    @pl.when(core == 0)
-    def _():
-        for k in Z_STEPS[:7]:
-            greet(at_z(k, 0)[1])
-            greet(at_z(k, 1)[1])
-
     for c in loads:
         c.start()
 
-    @pl.when(core == 0)
-    def _():
-        for k in Z_STEPS[7:]:
-            greet(at_z(k, 0)[1])
-            greet(at_z(k, 1)[1])
-
-    for k in Y_STEPS:
+    def greet_z(steps):
+        @pl.when(core == 0)
+        def _():
+            for k in steps:
+                greet(at_z(k, 0)[1])
+                greet(at_z(k, 1)[1])
+
+    greet_z(Z_STEPS[:7])
+    greet(at_y(4)[1])
+    greet_z(Z_STEPS[7:9])
+    for k in Y_STEPS[1:3]:
         greet(at_y(k)[1])
-    for k in X_STEPS:
+    greet_z(Z_STEPS[9:11])
+    greet(at_x(2)[1])
+    for k in Y_STEPS[3:5]:
+        greet(at_y(k)[1])
+    greet_z(Z_STEPS[11:13])
+    for k in Y_STEPS[5:]:
+        greet(at_y(k)[1])
+    for k in X_STEPS[1:]:
         greet(at_x(k)[1])
+    greet_z(Z_STEPS[13:])
     greet(sibling)
 
     @pl.when(core == 0)
@@ -207,7 +213,7 @@
             win[kind, c // NX, half * HID : (half + 1) * HID, col : col + LANES] = piece
 
     def send_y(rows):
-        for k in Y_STEPS:
+        for k in NEAR_FIRST:
             remote(rows.at[y, x], rows.at[y, x], gy_snd.at[k], gy_rcv.at[k], at_y(k)[1]).start()
 
     def send_x(rows, k, yy):
@@ -307,10 +313,9 @@
 
     def token_rows():
         back = z2_in[...].reshape(NZ * 8, LANES)
-        return lax.dot_general(
-            place[...], back, (((1,), (0,)), ((), ())),
-            precision=lax.Precision.HIGHEST, preferred_element_type=F32,
-        )
+        high = back.astype(BF)
+        low = (back - high.astype(F32)).astype(BF)
+        return nn_dot(place[...], high) + nn_dot(place[...], low)
 
     @pl.when(core == 0)
     def _():
@@ -319,7 +324,7 @@
         for c in swaps(shared_in, pre_s):
             c.start()
         z_in[0, z] = z_out[z]
-        place[...] = placing.T
+        place[...] = placing.T.astype(BF)
         z2_out[...] = jnp.zeros_like(z2_out)
         loaded = local_loads(routed_in, pre_r)
         for i in range(5):
@@ -327,14 +332,13 @@
         for i in range(3):
             window(i)
         pair_slots.wait_recv()
-        for k in range(1, NZ):
+        for k in Z_STEPS[::-1]:
             wait_slots(0, k)
             wait_slots(1, k)
         for b in range(NZ):
             slots[b * CAP : (b + 1) * CAP] = z_in[0, b, 0:CAP] + z_in[1, b, 0:CAP]
         rows_r[y, x] = slots[...].astype(BF)
         send_y(rows_r)
-        relay_x(rows_r)
         arrive = swaps(routed_in, pre_r)
         arrive[3].wait_recv()
         arrive[4].wait_recv()
@@ -342,6 +346,7 @@
         for i in range(3):
             arrive[i].wait_recv()
             window(3 + i)
+        relay_x(rows_r)
         dg, du = silu_grads(hidden(rows_r), factor_r)
         own_part(ROUTED, dg, du)
         slots[...] = reduce(ROUTED)
@@ -360,7 +365,7 @@
         slots_sent()
         pair.wait_send()
         answer.wait_recv()
-        for k in range(1, NZ):
+        for k in Z_STEPS[::-1]:
             wait_back(k, 0)
         out_ref[...] = (shared_sum[1] + token_rows()).T[0:FEAT].astype(BF)
         for k in range(1, NZ):
@@ -379,7 +384,7 @@
         send_y(rows_s)
         for c in swaps(routed_in, pre_r):
             c.start()
-        place[...] = placing.T
+        place[...] = placing.T.astype(BF)
         loaded = local_loads(shared_in, pre_s)
         for i in range(5):
             loaded[i].wait()
@@ -404,7 +409,7 @@
         pair_slots.wait_send()
         answer.wait_send()
         pair_back.wait_recv()
-        for k in range(1, NZ):
+        for k in Z_STEPS[::-1]:
             wait_back(k, 1)
         out_ref[...] = (shared_sum[0] + token_rows()).T[FEAT:CHUNK].astype(BF)
 
@@ -423,7 +428,7 @@
         pltpu.VMEM((2, ROUTED, 2 * HID), F32), pltpu.VMEM((2, TOK, 2 * HID), F32), pltpu.VMEM((2, TOK, LANES), BF),
         pltpu.VMEM((6, HID, WIDTH + LANES), BF),
         pltpu.VMEM((3, NY, 2 * HID, NX * LANES), BF),
-        pltpu.VMEM((TOK, NZ * 8), F32),
+        pltpu.VMEM((TOK, NZ * 8), BF),
         pltpu.VMEM((NZ, 8, LANES), F32), pltpu.VMEM((2, NZ, 8, LANES), F32),
         pltpu.VMEM((NZ, 8, LANES), F32), pltpu.VMEM((NZ, 8, LANES), F32),
         pltpu.VMEM((ROUTED, LANES), F32),

time: 64.8 us -> 64.1 us (0.989)
  Pallas kernels: 63.2 us -> 62.4 us
    pallas_call x1, Pallas kernels: 63.2 us -> 62.4 us  [body(): pl.pallas_call(kernel, out_shape=jax.ShapeDtypeStruct((FEAT, TOK), BF), i...]
where the time goes in v3:
time: 64.1 us; the launch traced here: 63.8 us
  Pallas kernels  62.4 us (97%)
  local copies, waits for them, and re-layouts  1.31 us (2%)
    pallas_call x1, Pallas kernels, body(): pl.pallas_call(kernel, out_shape=jax.ShapeDtypeStruct((FEAT, TOK), BF), i...  62.4 us
    unnamed x1, local copies, waits for them, and re-layouts  1.31 us

profile of v3, /device:TPU:1, one launch (start us, length us, event | category | flops | bytes accessed | tf_op | source)
XLA Modules:
  0.0 63.8 jit_solution(6641503303153748977)
XLA Ops:
  0.0 62.4 %shard_map.145 = bf16[50,64]{1,0:T(8,128)(2,1)} custom-call(bf16[50,64]{1,0:T(8,128)(2,1)} %bitcast.11, s32[1,64]{1,0:T(1,128)} %bitcast.12, s32[1,64]{1,0:T(1,128)} %bitcast.13, s32[1,16]{1,0:T(1,128)} %bitcast.14, f32[1,64]{1,0:T(1,128)} %bitcast.15, bf16[1,144,80]{2,1,0:T(8,128)(2,1)} %bitcast.9, bf16[1,144,80]{2,1,0:T(8,128)(2,1)} %bitcast.10, ...), custom_call_target="tpu_custom_call" | custom-call | tf_op jit(solution)/shard_map/pallas_call | solution.py:444
  62.5 1.3 %copy.17 = bf16[64,50]{0,1:T(8,128)(2,1)} copy(bf16[64,50]{0,1:T(8,128)(2,1)} %bitcast.8) | data formatting | bytes 12800

commit v4 on v3

--- a/solution.py
+++ b/solution.py
@@ -19,6 +19,8 @@
 LANES = 128
 WIDTH = CHIPS * CHUNK
 NEAR_FIRST = (1, 7, 2, 6, 3, 5, 4)
+SLOTS = (0,) + NEAR_FIRST
+BATCHES = ((0, 1), (1, 2), (3, 2), (5, 3))
 FAR_FIRST = (4, 3, 5, 2, 6, 1, 7, 0)
 X_STEPS = (2, 1, 3)
 Y_STEPS = (4, 3, 5, 2, 6, 1, 7)
@@ -212,37 +214,37 @@
             col = (c % NX) * LANES
             win[kind, c // NX, half * HID : (half + 1) * HID, col : col + LANES] = piece
 
+    def y_copy(rows, i):
+        k = SLOTS[i]
+        return remote(rows.at[x, 0], rows.at[x, i], gy_snd.at[k], gy_rcv.at[k], at_y(k)[1])
+
+    def x_copy(rows, b, j, xx):
+        part = rows.at[xx, pl.ds(*BATCHES[b])]
+        i = b * NX + j
+        return remote(part, part, gx_snd.at[i], gx_rcv.at[i], at_x(j)[1])
+
     def send_y(rows):
-        for k in NEAR_FIRST:
-            remote(rows.at[y, x], rows.at[y, x], gy_snd.at[k], gy_rcv.at[k], at_y(k)[1]).start()
-
-    def send_x(rows, k, yy):
-        for j in X_STEPS:
-            i = k * NX + j
-            remote(rows.at[yy, x], rows.at[yy, x], gx_snd.at[i], gx_rcv.at[i], at_x(j)[1]).start()
+        for i in range(1, NY):
+            y_copy(rows, i).start()
 
     def relay_x(rows):
-        send_x(rows, 0, y)
-        for k in NEAR_FIRST:
-            yy = lax.rem(y - k + NY, NY)
-            remote(rows.at[yy, x], rows.at[yy, x], gy_snd.at[k], gy_rcv.at[k], at_y(k)[1]).wait_recv()
-            send_x(rows, k, yy)
-
-    def row_of(rows, k):
-        yy = lax.rem(y - k + NY, NY)
-        for j in X_STEPS:
-            i = k * NX + j
-            xx = lax.rem(x - j + NX, NX)
-            remote(rows.at[yy, xx], rows.at[yy, xx], gx_snd.at[i], gx_rcv.at[i], at_x(j)[1]).wait_recv()
-        return yy
+        for b, (first, count) in enumerate(BATCHES):
+            for i in range(first, first + count):
+                if i:
+                    y_copy(rows, i).wait_recv()
+            for j in X_STEPS:
+                x_copy(rows, b, j, x).start()
 
     def hidden(rows):
         acc = None
-        for k in (0,) + NEAR_FIRST:
-            yy = row_of(rows, k)
-            wide = jnp.concatenate([rows[yy, j] for j in range(NX)], axis=1)
-            term = nt_dot(wide, win[0, yy])
-            acc = term if acc is None else acc + term
+        for b, (first, count) in enumerate(BATCHES):
+            for j in X_STEPS:
+                x_copy(rows, b, j, lax.rem(x - j + NX, NX)).wait_recv()
+            for i in range(first, first + count):
+                yy = lax.rem(y - SLOTS[i] + NY, NY)
+                wide = jnp.concatenate([rows[j, i] for j in range(NX)], axis=1)
+                term = nt_dot(wide, win[0, yy])
+                acc = term if acc is None else acc + term
         return acc
 
     def own_part(n, dg, du):
@@ -290,14 +292,15 @@
 
     def wait_sends(rows, n):
         for k in NEAR_FIRST:
-            remote(rows.at[y, x], rows.at[y, x], gy_snd.at[k], gy_rcv.at[k], at_y(k)[1]).wait_send()
+            y_copy(rows, SLOTS.index(k)).wait_send()
             remote(
                 y_out.at[k, pl.ds(0, n)], y_in.at[k, pl.ds(0, n)], ry_snd.at[k], ry_rcv.at[k], at_y(k)[1]
             ).wait_send()
         for k in range(NY):
             for j in X_STEPS:
                 i = k * NX + j
-                remote(rows.at[y, x], rows.at[y, x], gx_snd.at[i], gx_rcv.at[i], at_x(j)[1]).wait_send()
+                if k < len(BATCHES):
+                    x_copy(rows, k, j, x).wait_send()
                 remote(
                     sums.at[k, j, pl.ds(0, n)], x_in.at[k, j, pl.ds(0, n)],
                     rx_snd.at[i], rx_rcv.at[i], at_x(j)[1],
@@ -337,7 +340,7 @@
             wait_slots(1, k)
         for b in range(NZ):
             slots[b * CAP : (b + 1) * CAP] = z_in[0, b, 0:CAP] + z_in[1, b, 0:CAP]
-        rows_r[y, x] = slots[...].astype(BF)
+        rows_r[x, 0] = slots[...].astype(BF)
         send_y(rows_r)
         arrive = swaps(routed_in, pre_r)
         arrive[3].wait_recv()
@@ -380,7 +383,7 @@
         send_slots(1)
         pair_slots.start()
         pair.wait_recv()
-        rows_s[y, x] = placed[0] + placed[1]
+        rows_s[x, 0] = placed[0] + placed[1]
         send_y(rows_s)
         for c in swaps(routed_in, pre_r):
             c.start()
@@ -432,7 +435,7 @@
         pltpu.VMEM((NZ, 8, LANES), F32), pltpu.VMEM((2, NZ, 8, LANES), F32),
         pltpu.VMEM((NZ, 8, LANES), F32), pltpu.VMEM((NZ, 8, LANES), F32),
         pltpu.VMEM((ROUTED, LANES), F32),
-        pltpu.VMEM((NY, NX, ROUTED, LANES), BF), pltpu.VMEM((NY, NX, TOK, LANES), BF),
+        pltpu.VMEM((NX, NY, ROUTED, LANES), BF), pltpu.VMEM((NX, NY, TOK, LANES), BF),
         pltpu.VMEM((NX, ROUTED, LANES), F32), pltpu.VMEM((NY, ROUTED, LANES), F32),
         pltpu.VMEM((NY, NX, ROUTED, LANES), BF), pltpu.VMEM((NY, NX, ROUTED, LANES), BF),
         pltpu.VMEM((NY, ROUTED, LANES), BF), pltpu.VMEM((NY, ROUTED, LANES), BF),

time: 64.1 us -> 64.8 us (1.011)
  Pallas kernels: 62.4 us -> 63.1 us
    pallas_call x1, Pallas kernels: 62.4 us -> 63.1 us  [body(): pl.pallas_call(kernel, out_shape=jax.ShapeDtypeStruct((FEAT, TOK), BF), i...]
where the time goes in v4:
time: 64.8 us; the launch traced here: 64.5 us
  Pallas kernels  63.1 us (97%)
  local copies, waits for them, and re-layouts  1.31 us (2%)
    pallas_call x1, Pallas kernels, body(): pl.pallas_call(kernel, out_shape=jax.ShapeDtypeStruct((FEAT, TOK), BF), i...  63.1 us
    unnamed x1, local copies, waits for them, and re-layouts  1.31 us

profile of v4, /device:TPU:1, one launch (start us, length us, event | category | flops | bytes accessed | tf_op | source)
XLA Modules:
  0.0 64.5 jit_solution(16764766158503326962)
XLA Ops:
  0.0 63.1 %shard_map.145 = bf16[50,64]{1,0:T(8,128)(2,1)} custom-call(bf16[50,64]{1,0:T(8,128)(2,1)} %bitcast.11, s32[1,64]{1,0:T(1,128)} %bitcast.12, s32[1,64]{1,0:T(1,128)} %bitcast.13, s32[1,16]{1,0:T(1,128)} %bitcast.14, f32[1,64]{1,0:T(1,128)} %bitcast.15, bf16[1,144,80]{2,1,0:T(8,128)(2,1)} %bitcast.9, bf16[1,144,80]{2,1,0:T(8,128)(2,1)} %bitcast.10, ...), custom_call_target="tpu_custom_call" | custom-call | tf_op jit(solution)/shard_map/pallas_call | solution.py:447
  63.2 1.3 %copy.17 = bf16[64,50]{0,1:T(8,128)(2,1)} copy(bf16[64,50]{0,1:T(8,128)(2,1)} %bitcast.8) | data formatting | bytes 12800
